TPU v7x, 32 devices: a whole 2x2x4 slice. The times are simulated.
32 devices in a mesh: row: 8 (over y, x, core), col: 4 (over z).
Axes of the slice: x: 2, y: 2, z: 4, core: 2. Of those that a mesh axis runs over, the one named last changes fastest.
Arguments:
- x_tiles: bfloat16 [128, 8, 256, 256], P(('row', 'col')), as said below
- columns: int32 [128, 8], P(('row', 'col')), may hold values from 0 to 127, as said below
- branch: int32 [8, 2], P('row'), may hold values from 0 to 1
Outputs:
- purified: float32 [128, 8, 256, 256], P(('row', 'col'))
- occupation: float32 [8], P('row')
Inputs may be any that keep to these rules, and one draw needn't show every extreme that they name: `columns`: block rows form fragments of 16 consecutive rows, each with two halves of 8 rows. Slot 0 of a block row is the row itself; its other slots hold, in ascending order, every row of the other half of its fragment but one, so that the pattern is symmetric and no two rows of one half are coupled. `x_tiles`: every tile of the pattern is the transpose of its mirror tile, and diagonal tiles are symmetric.
All inputs are finite; a program needn't handle non-finite values.
Results may differ from a plain program's by a relative error of at most 0.0028.
Values may be sent and summed in bfloat16 or wider, within the bound.
A program may use at most 128 MiB of HBM per device.

v0:
```python
import jax
import jax.numpy as jnp
from jax import lax
from jax.sharding import PartitionSpec as P


def gather_partner_terms(rounded, partner):
    diagonal = rounded[:, 0]
    others = rounded[:, 1:]
    pieces = lax.all_gather(diagonal, "col", axis=0, tiled=True)
    width = pieces.shape[0]
    weights = (partner[:, :, None] == jnp.arange(width, dtype=jnp.int32)).astype(jnp.bfloat16)
    chosen = jnp.einsum(
        "bsm,mjk->bsjk", weights, pieces, preferred_element_type=jnp.float32
    ).astype(jnp.bfloat16)
    product = jnp.einsum("bsij,bskj->bsik", others, chosen, preferred_element_type=jnp.float32)
    return lax.optimization_barrier(product.astype(jnp.bfloat16)).astype(jnp.float32)


def shards(x_tiles, columns, branch):
    rows_dev = x_tiles.shape[0]
    tile_size = x_tiles.shape[2]
    col_count = lax.axis_size("col")
    cluster_rows = rows_dev * col_count
    local_cols = columns % cluster_rows
    partner = local_cols[:, 1:]
    identity = jnp.eye(tile_size, dtype=jnp.float32)
    current = x_tiles.astype(jnp.float32)
    for iteration in range(branch.shape[1]):
        step_sign = (2 * branch[0, iteration] - 1).astype(jnp.float32)
        rounded = current.astype(jnp.bfloat16)
        diagonal_sum = jnp.einsum(
            "btij,btkj->bik", rounded, rounded, preferred_element_type=jnp.float32
        )
        local_term = jnp.einsum(
            "bij,bsjk->bsik", rounded[:, 0], rounded[:, 1:], preferred_element_type=jnp.float32
        )
        partner_term = gather_partner_terms(rounded, partner)
        new_diagonal = current[:, 0] + step_sign * (diagonal_sum - 0.25 * identity)
        new_others = current[:, 1:] + step_sign * (local_term + partner_term)
        current = jnp.concatenate([new_diagonal[:, None], new_others], axis=1)
    trace_sum = jnp.sum(jnp.diagonal(current[:, 0], axis1=1, axis2=2))
    summed = lax.psum(trace_sum, "col")
    occupation = (summed / (cluster_rows * tile_size) + 0.5).reshape(1)
    return (current, occupation)


def solution(mesh):
    placed = (P(("row", "col"), None, None, None), P(("row", "col"), None), P("row", None))
    return jax.shard_map(
        shards,
        mesh=mesh,
        in_specs=placed,
        out_specs=(P(("row", "col"), None, None, None), P("row")),
        check_vma=False,
    )
```

profile of v0, /device:TPU:0, one launch (start us, length us, event | category | flops | bytes accessed | tf_op | source)
XLA Modules:
  0.0 176.2 jit_solution(16476128119525767314)
XLA Ops:
  7.2 6.7 %fusion.39 = (bf16[4,8,256,256]{3,2,0,1:T(8,128)(2,1)S(1)}, f32[4,8,256,256]{3,2,0,1:T(8,128)}) fusion(bf16[4,8,256,256]{3,2,1,0:T(8,128)(2,1)} %param.3), kind=kLoop, calls=%fused_computation.48 | loop fusion | flops 2097152 | bytes 16777216 | tf_op args[0]
  13.9 2.0 %copy-done.2 = bf16[4,8,256,256]{3,2,0,1:T(8,128)(2,1)} copy-done((bf16[4,8,256,256]{3,2,0,1:T(8,128)(2,1)}, bf16[4,8,256,256]{3,2,0,1:T(8,128)(2,1)S(1)}, u32[]{:S(2)}) %copy-start.2) | copy-done | bytes 4194328
  15.9 0.9 slice_bitcast_fusion.1
  16.8 0.0 all-gather.4.cloned.1.call-start
  16.8 0.6 fusion.40
  18.0 6.2 %fusion.42 = (bf16[4,256,256]{2,1,0:T(8,128)(2,1)}, f32[4,256,256]{2,1,0:T(8,128)}) fusion(f32[256,256]{1,0:T(8,128)S(1)} %fusion.31, bf16[4,8,256,256]{3,2,1,0:T(8,128)(2,1)} %param.3, f32[]{:T(128)} %bitcast.1, f32[4,8,256,256]{3,2,0,1:T(8,128)} %get-tuple-element.9), kind=kOutput, calls=%fused_computation.51 | convolution fusion | flops 1074790400 | bytes 11272704 | tf_op jit(solution)/shard_map/btij,btkj->bik/dot_general | solution.py:32
  24.3 4.3 %slice.33 = bf16[4,7,256,256]{3,2,1,0:T(8,128)(2,1)} slice(bf16[4,8,256,256]{3,2,1,0:T(8,128)(2,1)} %param.3), slice={[0:4], [1:8], [0:256], [0:256]} | slice | bytes 7340032 | tf_op jit(solution)/shard_map/slice | solution.py:36
  28.6 0.1 slice.35
  28.7 6.2 %copy.63 = bf16[4,7,256,256]{2,3,0,1:T(8,128)(2,1)} copy(bf16[4,7,256,256]{3,2,1,0:T(8,128)(2,1)} %slice.33) | data formatting | bytes 7340032
  35.6 30.0 %all-gather.6.cloned.1.call-done = bf16[16,1,256,256]{3,2,1,0:T(8,128)(2,1)} async-done(((bf16[4,1,256,256]{3,2,1,0:T(8,128)(2,1)}), bf16[16,1,256,256]{3,2,1,0:T(8,128)(2,1)}) %all-gather.6.cloned.1.call-update) | async-done | bytes 2097168 | tf_op jit(solution)/shard_map/all_gather | solution.py:10
  65.6 5.4 %convolution_convert_fusion.1 = bf16[4,7,256,256]{3,1,2,0:T(8,128)(2,1)} fusion(bf16[16,1,256,256]{3,2,1,0:T(8,128)(2,1)} %all-gather.6.cloned.1.call-done, s32[4,7]{1,0:T(4,128)S(1)} %slice.35), kind=kOutput, calls=%fused_computation.18 | convolution fusion | flops 60555712 | bytes 5767280 | tf_op jit(solution)/shard_map/bsm,mjk->bsjk/dot_general | solution.py:13
  71.0 4.6 %convert_bitcast_fusion = bf16[4,7,256,256]{3,2,0,1:T(8,128)(2,1)S(1)} fusion(bf16[4,7,256,256]{2,3,0,1:T(8,128)(2,1)S(1)} %copy-done.1, bf16[4,7,256,256]{3,1,2,0:T(8,128)(2,1)} %convolution_convert_fusion.1), kind=kOutput, calls=%fused_computation.16 | convolution fusion | flops 941359104 | bytes 11010048 | tf_op jit(solution)/shard_map/bsij,bskj->bsik/dot_general | solution.py:16
  75.6 6.9 %fusion.41 = (bf16[4,7,256,256]{3,2,0,1:T(8,128)(2,1)}, f32[4,7,256,256]{3,2,0,1:T(8,128)}) fusion(bf16[4,7,256,256]{3,2,0,1:T(8,128)(2,1)S(1)} %convert_bitcast_fusion, bf16[4,7,256,256]{2,3,0,1:T(8,128)(2,1)S(1)} %copy-done.1, bf16[4,8,256,256]{3,2,0,1:T(8,128)(2,1)} %copy-done.2, f32[]{:T(128)} %bitcast.1, f32[4,8,256,256]{3,2,0,1:T(8,128)S(1)} %bitcast.68), kind=kOutput, calls=%fused_computation.50 | convolution fusion | flops 948699136 | bytes 26214912 | tf_op jit(solution)/shard_map/bij,bsjk->bsik/dot_general | solution.py:35
  82.6 29.2 %all-gather.4.cloned.1.call-done = bf16[16,256,256]{2,1,0:T(8,128)(2,1)} async-done(((bf16[4,256,256]{2,1,0:T(8,128)(2,1)}), bf16[16,256,256]{2,1,0:T(8,128)(2,1)}) %all-gather.4.cloned.1.call-update) | async-done | bytes 2097168 | tf_op jit(solution)/shard_map/all_gather | solution.py:10
  111.8 3.4 %convolution_convert_fusion = bf16[4,7,256,256]{3,1,2,0:T(8,128)(2,1)S(1)} fusion(bf16[16,256,256]{2,1,0:T(8,128)(2,1)} %all-gather.4.cloned.1.call-done, s32[4,7]{1,0:T(4,128)S(1)} %slice.35), kind=kOutput, calls=%fused_computation.17 | convolution fusion | flops 60555712 | bytes 5767280 | tf_op jit(solution)/shard_map/bsm,mjk->bsjk/dot_general | solution.py:13
  115.3 3.3 %fusion.13 = bf16[4,7,256,256]{3,2,0,1:T(8,128)(2,1)} fusion(bf16[4,7,256,256]{3,2,0,1:T(8,128)(2,1)S(1)} %copy-done, bf16[4,7,256,256]{3,1,2,0:T(8,128)(2,1)S(1)} %convolution_convert_fusion), kind=kOutput, calls=%fused_computation.19 | convolution fusion | flops 941359104 | bytes 11010048 | tf_op jit(solution)/shard_map/bsij,bskj->bsik/dot_general | solution.py:16
  118.6 1.4 multiply_add_fusion
  120.0 16.5 %copy.48 = f32[4,256,256]{0,2,1:T(8,128)} copy(f32[4,256,256]{2,1,0:T(8,128)S(1)} %multiply_add_fusion) | data formatting | bytes 2097152 | tf_op jit(solution)/shard_map/add | solution.py:39
  136.4 6.3 %fusion.1 = f32[4,7,256,256]{3,2,0,1:T(8,128)S(1)} fusion(f32[4,7,256,256]{3,2,0,1:T(8,128)} %get-tuple-element.13, bf16[4,7,256,256]{3,2,0,1:T(8,128)(2,1)} %fusion.13, f32[]{:T(128)} %bitcast.4, bf16[4,7,256,256]{3,2,0,1:T(8,128)(2,1)} %get-tuple-element.12, bf16[4,256,256]{2,1,0:T(8,128)(2,1)S(1)} %copy-done.3), kind=kOutput, calls=%fused_computation.5 | convolution fusion | flops 946864128 | bytes 22544388 | tf_op jit(solution)/shard_map/bij,bsjk->bsik/dot_general | solution.py:35
  142.8 4.2 %pad_maximum_fusion = f32[4,8,256,256]{3,2,0,1:T(8,128)} fusion(f32[4,7,256,256]{3,2,0,1:T(8,128)S(1)} %fusion.1, f32[4,1,256,256]{3,2,0,1:T(8,128)S(1)} %bitcast.71), kind=kLoop, calls=%fused_computation.1 | loop fusion | flops 2097152 | bytes 16777216 | tf_op jit(solution)/shard_map/concatenate | solution.py:41
  146.9 2.3 %gather_fusion = f32[256,4]{1,0:T(8,128)S(1)} fusion(f32[4,256,256]{0,2,1:T(8,128)} %copy.48, s32[256]{0:T(256)S(1)} %bitcast.69), kind=kCustom, calls=%fused_computation | custom fusion | bytes 10240 | tf_op jit(solution)/shard_map/jit(diagonal)/gather | solution.py:42
  149.2 0.6 reduce_sum.9
  149.9 7.7 %copy.49 = f32[4,8,256,256]{3,2,1,0:T(8,128)} copy(f32[4,8,256,256]{3,2,0,1:T(8,128)} %pad_maximum_fusion) | data formatting | bytes 16777216
  157.5 10.1 %psum.7 = f32[]{:T(128)} all-reduce(f32[]{:T(128)} %reduce_sum.9), channel_id=1, replica_groups=mesh['row'=8,'col'=4] {'col'}, use_global_device_ids=true, to_apply=%region_1.2 | all-reduce | flops 1 | bytes 8 | tf_op jit(solution)/shard_map/psum | solution.py:43
  (24 shorter events, 0.1 us)
Async XLA Ops:
  7.2 9.7 %copy-start.6 = (s32[1,2]{1,0:T(1,128)S(1)}, s32[1,2]{1,0:T(1,128)}, u32[]{:S(2)}) copy-start(s32[1,2]{1,0:T(1,128)} %param.5) | copy-start | bytes 28
  7.2 58.4 %all-gather.6.cloned.1.call-start = ((), (), s32[]{:S(2)}) async-start(), calls=%async_computation.1 | async-start | bytes 2621440 | tf_op jit(solution)/shard_map/all_gather | solution.py:10
  13.9 2.0 %copy-start.2 = (bf16[4,8,256,256]{3,2,0,1:T(8,128)(2,1)}, bf16[4,8,256,256]{3,2,0,1:T(8,128)(2,1)S(1)}, u32[]{:S(2)}) copy-start(bf16[4,8,256,256]{3,2,0,1:T(8,128)(2,1)S(1)} %get-tuple-element.8) | copy-start | bytes 12582916
  16.8 95.0 %all-gather.4.cloned.1.call-start = ((), (), s32[]{:S(2)}) async-start(), calls=%async_computation | async-start | bytes 2621440 | tf_op jit(solution)/shard_map/all_gather | solution.py:10
  24.2 4.3 %copy-start.5 = (s32[4,8]{1,0:T(4,128)S(1)}, s32[4,8]{1,0:T(4,128)}, u32[]{:S(2)}) copy-start(s32[4,8]{1,0:T(4,128)} %param.4) | copy-start | bytes 388
  65.6 5.4 %copy-start.1 = (bf16[4,7,256,256]{2,3,0,1:T(8,128)(2,1)S(1)}, bf16[4,7,256,256]{2,3,0,1:T(8,128)(2,1)}, u32[]{:S(2)}) copy-start(bf16[4,7,256,256]{2,3,0,1:T(8,128)(2,1)} %copy.63) | copy-start | bytes 11010052
  65.6 10.0 %slice-start = ((s8[8388608]{0:T(1024)(128)(4,1)}), s8[4194304]{0:T(1024)(128)(4,1)S(1)}, s32[]{:S(2)}) async-start(s8[8388608]{0:T(1024)(128)(4,1)} %bitcast.67), calls=%async_computation.2 | async-start | bytes 8388608
  71.0 4.7 %slice-start.1 = ((s8[8388608]{0:T(1024)(128)(4,1)}), s8[4194304]{0:T(1024)(128)(4,1)S(1)}, s32[]{:S(2)}) async-start(s8[8388608]{0:T(1024)(128)(4,1)} %bitcast.67), calls=%async_computation.3 | async-start | bytes 8388608
  111.8 3.4 %copy-start = (bf16[4,7,256,256]{3,2,0,1:T(8,128)(2,1)S(1)}, bf16[4,7,256,256]{3,2,0,1:T(8,128)(2,1)}, u32[]{:S(2)}) copy-start(bf16[4,7,256,256]{3,2,0,1:T(8,128)(2,1)} %get-tuple-element.12) | copy-start | bytes 11010052
  115.3 3.3 %copy-start.3 = (bf16[4,256,256]{2,1,0:T(8,128)(2,1)S(1)}, bf16[4,256,256]{2,1,0:T(8,128)(2,1)}, u32[]{:S(2)}) copy-start(bf16[4,256,256]{2,1,0:T(8,128)(2,1)} %get-tuple-element.14) | copy-start | bytes 1572868
  115.3 3.3 %copy-start.4 = (f32[4,256,256]{2,1,0:T(8,128)S(1)}, f32[4,256,256]{2,1,0:T(8,128)}, u32[]{:S(2)}) copy-start(f32[4,256,256]{2,1,0:T(8,128)} %get-tuple-element.15) | copy-start | bytes 3145732
Sparse Core Ops, SparseCore 0:
  16.9 48.6 all-gather.5
  67.1 44.6 all-gather.3
where the time goes:
time: 177 us; the launch traced here: 176 us
  waiting for transfers between devices  59.3 us (34%)
  local copies, waits for them, and re-layouts  40.5 us (23%)
  matrix products  37.6 us (21%)
  between operations  17.2 us (10%)
  other arithmetic  11.5 us (6%)
  blocking collectives  10.1 us (6%)
    all_gather x2, waiting for transfers between devices, gather_partner_terms(): pieces = lax.all_gather(diagonal, 'col', axis=0, tiled=True)  59.2 us
    add x1, local copies, waits for them, and re-layouts, shards(): new_diagonal = current[:, 0] + step_sign * (diagonal_sum - 0.25 * identity)  16.5 us
    unnamed x20, local copies, waits for them, and re-layouts  15.9 us
    dot_general x2, matrix products, shards(): jnp.einsum('bij,bsjk->bsik', rounded[:, 0], rounded[:, 1:], preferred_ele...  13.2 us
    psum x1, blocking collectives, shards(): summed = lax.psum(trace_sum, 'col')  10.1 us
    dot_general x2, matrix products, gather_partner_terms(): jnp.einsum('bsm,mjk->bsjk', weights, pieces, preferred_element_type=jnp.f...  8.83 us
    dot_general x2, matrix products, gather_partner_terms(): jnp.einsum('bsij,bskj->bsik', others, chosen, preferred_element_type=jnp....  7.94 us
    dot_general x2, matrix products, shards(): jnp.einsum('btij,btkj->bik', rounded, rounded, preferred_element_type=jnp...  7.6 us
  transfers between devices with their start and end apart: 2, of which 2 were waited for; matrix products, arithmetic and copies ran while one was open for 20% of the time, Pallas kernels for 0%

commit v1 on v0

v1 whole, which is shorter than its diff:
```python
import functools

import jax
import jax.numpy as jnp
from jax import lax
from jax.experimental import pallas as pl
from jax.experimental.pallas import tpu as pltpu
from jax.sharding import PartitionSpec as P

MESH = pl.DeviceIdType.MESH
HEAD = 16
NN = (((1,), (0,)), ((), ()))
NT = (((1,), (1,)), ((), ()))


def mm(a, b, dims=NN):
    return lax.dot_general(a, b, dims, preferred_element_type=jnp.float32)


def purify_kernel(
    n, cols_ref, branch_ref, x_hbm, out_ref, occ_ref,
    x, d1, send, recv, gath, trace, load_sem, send_sem, recv_sem, pass_sem, tsend_sem, trecv_sem,
):
    rows, slots, size = x.shape[0], x.shape[1], x.shape[2]
    half_tile = size // 2
    h = n // 2
    half_rows = rows * h
    me = lax.axis_index("col")
    upper = (me >= h).astype(jnp.int32)
    mine = me - upper * h
    dist = jnp.where(me < h, h - 1 - me, me - h)
    target = jnp.where(me < h, h, h - 1)
    onward = jnp.where(me < h, me - 1, me + 1)

    load_diag = pltpu.make_async_copy(x_hbm.at[:, 0:1], x.at[:, 0:1], load_sem.at[0])
    load_rest = pltpu.make_async_copy(x_hbm.at[:, 1:slots], x.at[:, 1:slots], load_sem.at[1])
    load_diag.start()
    load_rest.start()

    barrier = pltpu.get_barrier_semaphore()
    for k in range(1, n):
        pl.semaphore_signal(barrier, inc=1, device_id={"col": lax.rem(me + k, n)}, device_id_type=MESH)

    signs = [(2 * branch_ref[0, step] - 1).astype(jnp.float32) for step in range(2)]
    ri = lax.broadcasted_iota(jnp.int32, (half_tile, half_tile), 0)
    ci = lax.broadcasted_iota(jnp.int32, (half_tile, half_tile), 1)
    head_row = lax.broadcasted_iota(jnp.int32, (HEAD, half_tile), 0)
    eye = (
        lax.broadcasted_iota(jnp.int32, (size, size), 0) == lax.broadcasted_iota(jnp.int32, (size, size), 1)
    )

    def chunk(t):
        return (0, HEAD + size) if t == 0 else (HEAD + t * size, size)

    def pack(tile, step, t, head):
        a11 = tile[:half_tile, :half_tile]
        a22 = tile[half_tile:, half_tile:]
        at = pl.multiple_of(HEAD + t * size, HEAD)
        send[step, pl.ds(at, half_tile), :] = jnp.where(ri <= ci, a11, a22).astype(jnp.bfloat16)
        send[step, pl.ds(at + half_tile, half_tile), :] = tile[:half_tile, half_tile:].astype(jnp.bfloat16)
        corner = jnp.sum(jnp.where(ri == ci, a22, 0.0), axis=0, keepdims=True)
        return head + jnp.where(head_row == t, corner, 0.0)

    def own_copy(step, t):
        at, length = chunk(t)
        return pltpu.make_async_remote_copy(
            src_ref=send.at[step, pl.ds(at, length)],
            dst_ref=recv.at[step, mine, pl.ds(at, length)],
            send_sem=send_sem.at[step, t],
            recv_sem=recv_sem.at[step, mine, t],
            device_id={"col": target},
            device_id_type=MESH,
        )

    def pass_copy(step, r, t):
        at, length = chunk(t)
        return pltpu.make_async_remote_copy(
            src_ref=recv.at[step, r, pl.ds(at, length)],
            dst_ref=recv.at[step, r, pl.ds(at, length)],
            send_sem=pass_sem.at[step, r, t],
            recv_sem=recv_sem.at[step, r, t],
            device_id={"col": onward},
            device_id_type=MESH,
        )

    def arrive(step, t):
        for r in range(h):
            pass_copy(step, r, t).wait_recv()

            @pl.when(dist < h - 1)
            def _():
                pass_copy(step, r, t).start()

    def unpack(step, t):
        for r in range(h):
            at = HEAD + t * size
            mixed = recv[step, r, pl.ds(at, half_tile), :].astype(jnp.float32)
            cross = recv[step, r, pl.ds(at + half_tile, half_tile), :]
            head = recv[step, r, 0:HEAD, :].astype(jnp.float32)
            corner = jnp.sum(jnp.where(head_row == t, head, 0.0), axis=0, keepdims=True)
            turned = mixed.T
            a11 = jnp.where(ri <= ci, mixed, turned)
            a22 = jnp.where(ri > ci, mixed, jnp.where(ri == ci, corner, turned))
            g = r * rows + t
            gath[step, g, 0:half_tile, 0:half_tile] = a11.astype(jnp.bfloat16)
            gath[step, g, half_tile:, half_tile:] = a22.astype(jnp.bfloat16)
            gath[step, g, 0:half_tile, half_tile:] = cross
            gath[step, g, half_tile:, 0:half_tile] = cross.astype(jnp.float32).T.astype(jnp.bfloat16)

    def ready(t):
        return [
            s for s in range(slots - 1)
            if max(s % rows, (s + 1) % rows) == t
        ]

    def other(step, i, s):
        first = lax.rem(cols_ref[i, s + 1], half_rows) == s
        return lax.select(first, gath[step, s], gath[step, s + 1])

    load_diag.wait()
    head = jnp.zeros((HEAD, half_tile), jnp.float32)
    for t in range(rows):
        head = pack(x[t, 0].astype(jnp.float32), 0, t, head)
    send[0, 0:HEAD, :] = head.astype(jnp.bfloat16)
    pl.semaphore_wait(barrier, n - 1)
    for t in range(rows):
        own_copy(0, t).start()

    load_rest.wait()

    def first_diagonal(i, head):
        total = mm(x[i, 0], x[i, 0], NT)
        for s in range(1, slots):
            total += mm(x[i, s], x[i, s], NT)
        new = x[i, 0].astype(jnp.float32) + signs[0] * (total - jnp.where(eye, 0.25, 0.0))
        out_ref[i, 0] = new
        d1[i, 0] = new.astype(jnp.bfloat16)
        return pack(new, 1, i, head)

    head = lax.fori_loop(0, rows, first_diagonal, jnp.zeros((HEAD, half_tile), jnp.float32))
    send[1, 0:HEAD, :] = head.astype(jnp.bfloat16)
    for t in range(rows):
        own_copy(1, t).start()

    def first_local(i, carry):
        for s in range(1, slots):
            out_ref[i, s] = x[i, s].astype(jnp.float32) + signs[0] * mm(x[i, 0], x[i, s])
        return carry

    lax.fori_loop(0, rows, first_local, 0)

    for t in range(rows):
        arrive(0, t)
        unpack(0, t)
        todo = ready(t)

        def first_partner(i, carry):
            for s in todo:
                new = out_ref[i, s + 1] + signs[0] * mm(x[i, s + 1], other(0, i, s))
                low = new.astype(jnp.bfloat16)
                d1[i, s + 1] = low
                out_ref[i, s + 1] = new + signs[1] * mm(d1[i, 0], low)
            return carry

        if todo:
            lax.fori_loop(0, rows, first_partner, 0)

    arrive(1, 0)
    unpack(1, 0)

    def second_diagonal(i, carry):
        total = mm(d1[i, 0], d1[i, 0], NT)
        for s in range(1, slots):
            total += mm(d1[i, s], d1[i, s], NT)
        new = out_ref[i, 0] + signs[1] * (total - jnp.where(eye, 0.25, 0.0))
        out_ref[i, 0] = new
        on_diag = jnp.where(eye, new, 0.0)
        return carry + jnp.sum(jnp.sum(on_diag.reshape(size // 8, 8, 2, half_tile), axis=0), axis=1)

    lanes = lax.fori_loop(0, rows, second_diagonal, jnp.zeros((8, half_tile), jnp.float32))
    trace[me] = lanes

    def trace_copy(k):
        return pltpu.make_async_remote_copy(
            src_ref=trace.at[me],
            dst_ref=trace.at[me],
            send_sem=tsend_sem.at[k],
            recv_sem=trecv_sem.at[k],
            device_id={"col": lax.rem(me + k, n)},
            device_id_type=MESH,
        )

    def trace_landing(k):
        source = lax.rem(me + n - k, n)
        return pltpu.make_async_remote_copy(
            src_ref=trace.at[source],
            dst_ref=trace.at[source],
            send_sem=tsend_sem.at[k],
            recv_sem=trecv_sem.at[k],
            device_id={"col": lax.rem(me + k, n)},
            device_id_type=MESH,
        )

    for k in range(1, n):
        trace_copy(k).start()

    for t in range(rows):
        if t > 0:
            arrive(1, t)
            unpack(1, t)
        todo = ready(t)

        def second_partner(i, carry):
            for s in todo:
                out_ref[i, s + 1] = out_ref[i, s + 1] + signs[1] * mm(d1[i, s + 1], other(1, i, s))
            return carry

        if todo:
            lax.fori_loop(0, rows, second_partner, 0)

    for k in range(1, n):
        trace_landing(k).wait_recv()
        trace_copy(k).wait_send()
    total = trace[0]
    for k in range(1, n):
        total = total + trace[k]
    scale = 1.0 / (rows * n * size)
    occ_ref[...] = jnp.broadcast_to(jnp.sum(total, keepdims=True) * scale + 0.5, occ_ref.shape)

    for step in range(2):
        for t in range(rows):
            own_copy(step, t).wait_send()

    @pl.when(dist < h - 1)
    def _():
        for step in range(2):
            for r in range(h):
                for t in range(rows):
                    pass_copy(step, r, t).wait_send()


def write_kernel(held, out_hbm, sem):
    copies = [
        pltpu.make_async_copy(held.at[i], out_hbm.at[i], sem.at[i]) for i in range(held.shape[0])
    ]
    for copy in copies:
        copy.start()
    for copy in copies:
        copy.wait()


def shards(n, x_tiles, columns, branch):
    rows, slots, size = x_tiles.shape[0], x_tiles.shape[1], x_tiles.shape[2]
    h = n // 2
    length = HEAD + rows * size
    vmem = pl.BlockSpec(memory_space=pltpu.VMEM)
    smem = pl.BlockSpec(memory_space=pltpu.SMEM)
    flops = 2 * size**3 * rows * (slots * 2 + (slots - 1) * 4)
    held, occ = pl.pallas_call(
        functools.partial(purify_kernel, n),
        out_shape=(
            pltpu.VMEM(x_tiles.shape, jnp.float32),
            jax.ShapeDtypeStruct((8, 128), jnp.float32),
        ),
        in_specs=[smem, smem, pl.BlockSpec(memory_space=pltpu.HBM)],
        out_specs=(vmem, vmem),
        scratch_shapes=[
            pltpu.VMEM((rows, slots, size, size), jnp.bfloat16),
            pltpu.VMEM((rows, slots, size, size), jnp.bfloat16),
            pltpu.VMEM((2, length, size // 2), jnp.bfloat16),
            pltpu.VMEM((2, h, length, size // 2), jnp.bfloat16),
            pltpu.VMEM((2, h * rows, size, size), jnp.bfloat16),
            pltpu.VMEM((n, 8, size // 2), jnp.float32),
            pltpu.SemaphoreType.DMA((2,)),
            pltpu.SemaphoreType.DMA((2, rows)),
            pltpu.SemaphoreType.DMA((2, h, rows)),
            pltpu.SemaphoreType.DMA((2, h, rows)),
            pltpu.SemaphoreType.DMA((n,)),
            pltpu.SemaphoreType.DMA((n,)),
        ],
        compiler_params=pltpu.CompilerParams(
            collective_id=0, has_side_effects=True, vmem_limit_bytes=40 * 2**20
        ),
        cost_estimate=pl.CostEstimate(flops=flops, bytes_accessed=3 * x_tiles.size * 2, transcendentals=0),
        name="purify",
    )(columns, branch, x_tiles)
    purified = pl.pallas_call(
        write_kernel,
        out_shape=jax.ShapeDtypeStruct(x_tiles.shape, jnp.float32),
        in_specs=[vmem],
        out_specs=pl.BlockSpec(memory_space=pl.ANY),
        scratch_shapes=[pltpu.SemaphoreType.DMA((rows,))],
        cost_estimate=pl.CostEstimate(flops=0, bytes_accessed=x_tiles.size * 4, transcendentals=0),
        name="write",
    )(held)
    return purified, occ[0, 0:1]


def solution(mesh):
    placed = (P(("row", "col"), None, None, None), P(("row", "col"), None), P("row", None))
    return jax.shard_map(
        functools.partial(shards, mesh.shape["col"]),
        mesh=mesh,
        in_specs=placed,
        out_specs=(P(("row", "col"), None, None, None), P("row")),
        check_vma=False,
    )
```

time: 177 us -> 60.9 us (0.34)
  waiting for transfers between devices: 59.3 us -> 0 us
  Pallas kernels: 0 us -> 52.8 us
  matrix products: 37.6 us -> 0 us
  local copies, waits for them, and re-layouts: 40.5 us -> 7.24 us
  between operations: 17.2 us -> 0.66 us
  other arithmetic: 11.5 us -> 0 us
  blocking collectives: 10.1 us -> 0 us
    all_gather x2 -> x0, waiting for transfers between devices: 59.2 us -> none  [gather_partner_terms(): pieces = lax.all_gather(diagonal, 'col', axis=0, tiled=True)]
    pallas_call x0 -> x2, Pallas kernels: none -> 52.8 us  [the longest x1 46 us: shards(): pl.pallas_call(functools.partial(purify_kernel, n), out_shape=(pltpu.VMEM...]
    dot_general x8 -> x0, matrix products: 37.6 us -> none  [the longest x2 13.2 us: shards(): jnp.einsum('bij,bsjk->bsik', rounded[:, 0], rounded[:, 1:], preferred_ele...]
    add x1 -> x0, local copies, waits for them, and re-layouts: 16.5 us -> none  [shards(): new_diagonal = current[:, 0] + step_sign * (diagonal_sum - 0.25 * identity)]
    psum x1 -> x0, blocking collectives: 10.1 us -> none  [shards(): summed = lax.psum(trace_sum, 'col')]
    unnamed x20 -> x8, local copies, waits for them, and re-layouts: 15.9 us -> 6.73 us
    unnamed x2 -> x0, other arithmetic: 6.7 us -> none
    slice x4 -> x1, local copies, waits for them, and re-layouts: 5.83 us -> 0.51 us  [shards(): return (purified, occ[0, 0:1])]
  transfers between devices with their start and end apart: 2 -> 0, of which waited for: 2 -> 0; matrix products, arithmetic and copies ran while one was open for 20% -> 0% of each run, Pallas kernels for 0% -> 0%
where the time goes in v1:
time: 60.9 us; the launch traced here: 60.6 us
  Pallas kernels  52.8 us (87%)
  local copies, waits for them, and re-layouts  7.24 us (12%)
  between operations  0.66 us (1%)
    pallas_call x1, Pallas kernels, shards(): pl.pallas_call(functools.partial(purify_kernel, n), out_shape=(pltpu.VMEM...  46 us
    pallas_call x1, Pallas kernels, shards(): pl.pallas_call(write_kernel, out_shape=jax.ShapeDtypeStruct(x_tiles.shape...  6.74 us
    unnamed x8, local copies, waits for them, and re-layouts  6.73 us

profile of v1, /device:TPU:0, one launch (start us, length us, event | category | flops | bytes accessed | tf_op | source)
XLA Modules:
  0.0 60.6 jit_solution(16961518200156598153)
XLA Ops:
  0.6 0.0 copy-start.1
  0.6 2.2 %copy-done.1 = bf16[4,8,256,256]{3,2,1,0:T(8,128)(2,1)S(1)} copy-done((bf16[4,8,256,256]{3,2,1,0:T(8,128)(2,1)S(1)}, bf16[4,8,256,256]{3,2,1,0:T(8,128)(2,1)}, u32[]{:S(2)}) %copy-start.1) | copy-done | bytes 4194328
  2.8 0.0 copy-start.2
  2.8 0.7 %copy-done.2 = s32[4,8]{1,0:T(4,128)S(1)} copy-done((s32[4,8]{1,0:T(4,128)S(1)}, s32[4,8]{1,0:T(4,128)}, u32[]{:S(2)}) %copy-start.2) | copy-done | bytes 152
  3.5 0.0 copy-start.3
  3.5 0.7 %copy-done.3 = s32[1,2]{1,0:T(1,128)S(1)} copy-done((s32[1,2]{1,0:T(1,128)S(1)}, s32[1,2]{1,0:T(1,128)}, u32[]{:S(2)}) %copy-start.3) | copy-done | bytes 32
  4.2 46.0 %purify.1 = (f32[4,8,256,256]{3,2,1,0:T(8,128)S(1)}, f32[8,128]{1,0:T(8,128)S(1)}) custom-call(s32[4,8]{1,0:T(4,128)S(1)} %copy-done.2, s32[1,2]{1,0:T(1,128)S(1)} %copy-done.3, bf16[4,8,256,256]{3,2,1,0:T(8,128)(2,1)S(1)} %copy-done.1), custom_call_target="tpu_custom_call" | custom-call | flops 5905580032 | bytes 12582912 | tf_op jit(solution)/shard_map/purify/pallas_call | solution.py:259
  50.2 0.0 copy-start
  50.2 3.2 %copy-done = f32[4,8,256,256]{3,2,1,0:T(8,128)} copy-done((f32[4,8,256,256]{3,2,1,0:T(8,128)}, f32[4,8,256,256]{3,2,1,0:T(8,128)S(1)}, u32[]{:S(2)}) %copy-start) | copy-done | bytes 8388632
  53.4 0.5 slice.3
  53.9 6.7 %write.1 = f32[4,8,256,256]{3,2,1,0:T(8,128)} custom-call(f32[4,8,256,256]{3,2,1,0:T(8,128)} %copy-done), custom_call_target="tpu_custom_call" | custom-call | bytes 8388608 | tf_op jit(solution)/shard_map/write/pallas_call | solution.py:287
Async XLA Ops:
  0.6 2.2 %copy-start.1 = (bf16[4,8,256,256]{3,2,1,0:T(8,128)(2,1)S(1)}, bf16[4,8,256,256]{3,2,1,0:T(8,128)(2,1)}, u32[]{:S(2)}) copy-start(bf16[4,8,256,256]{3,2,1,0:T(8,128)(2,1)} %x_hbm.1) | copy-start | bytes 12582916
  2.8 0.7 %copy-start.2 = (s32[4,8]{1,0:T(4,128)S(1)}, s32[4,8]{1,0:T(4,128)}, u32[]{:S(2)}) copy-start(s32[4,8]{1,0:T(4,128)} %cols_ref.1) | copy-start | bytes 388
  3.5 0.7 %copy-start.3 = (s32[1,2]{1,0:T(1,128)S(1)}, s32[1,2]{1,0:T(1,128)}, u32[]{:S(2)}) copy-start(s32[1,2]{1,0:T(1,128)} %branch_ref.1) | copy-start | bytes 28
  50.2 3.2 %copy-start = (f32[4,8,256,256]{3,2,1,0:T(8,128)}, f32[4,8,256,256]{3,2,1,0:T(8,128)S(1)}, u32[]{:S(2)}) copy-start(f32[4,8,256,256]{3,2,1,0:T(8,128)S(1)} %get-tuple-element.4.held) | copy-start | bytes 25165828
